TPU v7x, 512 devices: a whole 4x8x8 slice. The times are simulated.
512 devices in a mesh: dp: 16 (over y, core), seq: 32 (over x, z).
Axes of the slice: x: 4, y: 8, z: 8, core: 2. Of those that a mesh axis runs over, the one named last changes fastest.
Arguments:
- frame_in: bfloat16 [16, 4608, 1024], P('dp', 'seq'), may hold values from -120 to 120
- token_ids: int32 [16, 32, 60], P('dp', 'seq'), may hold values from 0 to 3327
- durations: int32 [16, 32, 60], P('dp', 'seq'), may hold values from 1 to 4, 144 in all within a row
- valid_len: int32 [16], P('dp'), may hold values from 1152 to 4608, as said below
- t_bin: int32 [16], P('dp'), may hold values from 0 to 63
- token_table: bfloat16 [3328, 512], P('seq'), may hold values from -6 to 6
- enc_weight: bfloat16 [512, 1024], replicated, may hold values from -0.25 to 0.25
- mod_table: float32 [64, 2048], replicated, may hold values from -1.2 to 2.5
- w_query: bfloat16 [1024, 512], P('seq'), may hold values from -0.1875 to 0.1875
- w_key: bfloat16 [1024, 512], P('seq'), may hold values from -0.1875 to 0.1875
- w_value: bfloat16 [1024, 512], P('seq'), may hold values from -0.1875 to 0.1875
- attn_grad: bfloat16 [16, 4608, 512], P('dp', 'seq'), may hold values from -6 to 6
Outputs:
- attn_out: bfloat16 [16, 4608, 512], P('dp', 'seq')
- frame_grad: bfloat16 [16, 4608, 1024], P('dp', 'seq')
- query_weight_grad: float32 [1024, 512], P('seq')
- key_weight_grad: float32 [1024, 512], P('seq')
- value_weight_grad: float32 [1024, 512], P('seq')
Inputs may be any that keep to these rules, and one draw needn't show every extreme that they name: In every slab the 60 durations sum to 144, so each token's frames lie in its own slab; some token lasts 4 frames. `valid_len`: some recording is valid over all 4608 frames.
All inputs are finite; a program needn't handle non-finite values.
Results may differ from a plain program's by a relative error of at most 0.017.
The roundings to bfloat16 on the way count: a program that leaves them out, or rounds other values in their place, can miss the bound.
Values may be sent and summed in bfloat16 or wider, within the bound.
A program may use at most 64 MiB of HBM per device.

v0:
```python
import math
import jax
import jax.numpy as jnp
from jax import lax
from jax.sharding import PartitionSpec as P

D = 1024
HEADS = 8
HD = 64
BLK = 48
QW = 512


def extended_2(cells, sides, width):
    for axis, dim in sides:
        count = lax.axis_size(axis)
        ends = count - 1
        head = lax.slice_in_dim(cells, 0, width, axis=dim)
        tail = lax.slice_in_dim(cells, cells.shape[dim] - width, cells.shape[dim], axis=dim)
        cells = jnp.concatenate(
            [
                lax.ppermute(tail, axis, [(i, (i + 1) % count) for i in range(ends)]),
                cells,
                lax.ppermute(head, axis, [((i + 1) % count, i) for i in range(ends)]),
            ],
            axis=dim,
        )
    return cells


def shifted(block, axis, distance):
    devices = range(lax.axis_size(axis))
    route = [(i - distance, i) for i in devices if i - distance in devices]
    return lax.ppermute(block, axis, route)


def attend_window(
    q_blocks, key_ext, value_ext, grad_out, query_pos, key_pos, valid_end, frames_total
):
    n_blocks = q_blocks.shape[0]
    block_len = q_blocks.shape[1]
    key_win = jnp.concatenate([key_ext[offset : offset + n_blocks] for offset in range(4)], axis=1)
    value_win = jnp.concatenate(
        [value_ext[offset : offset + n_blocks] for offset in range(4)], axis=1
    )
    key_here = key_pos[:, None, :]
    allowed = (
        (key_here >= 0)
        & (key_here < frames_total)
        & ((key_here < valid_end) | (query_pos[:, :, None] >= valid_end))
    )
    row_mask = allowed[:, None]
    inv_scale = 1.0 / math.sqrt(q_blocks.shape[-1])
    scores = (
        jnp.einsum("bqhd,bkhd->bhqk", q_blocks, key_win, preferred_element_type=jnp.float32)
        * inv_scale
    )
    scores = jnp.where(row_mask, scores, -1e30)
    row_top = jnp.max(scores, axis=-1, keepdims=True)
    shifted_exp = jnp.where(row_mask, jnp.exp(scores - row_top), 0.0)
    attn_prob = shifted_exp / jnp.sum(shifted_exp, axis=-1, keepdims=True)
    probs_low = attn_prob.astype(jnp.bfloat16)
    mixed_out = jnp.einsum(
        "bhqk,bkhd->bqhd", probs_low, value_win, preferred_element_type=jnp.float32
    ).astype(jnp.bfloat16)
    grad_probs = jnp.einsum(
        "bqhd,bkhd->bhqk", grad_out, value_win, preferred_element_type=jnp.float32
    )
    centre = jnp.sum(attn_prob * grad_probs, axis=-1, keepdims=True)
    grad_scores = (attn_prob * (grad_probs - centre) * inv_scale).astype(jnp.bfloat16)
    grad_query = jnp.einsum(
        "bhqk,bkhd->bqhd", grad_scores, key_win, preferred_element_type=jnp.float32
    ).astype(jnp.bfloat16)
    key_terms = jnp.einsum(
        "bhqk,bqhd->bkhd", grad_scores, q_blocks, preferred_element_type=jnp.float32
    )
    value_terms = jnp.einsum(
        "bhqk,bqhd->bkhd", probs_low, grad_out, preferred_element_type=jnp.float32
    )
    win_terms = jnp.concatenate([key_terms, value_terms], axis=2)
    pieces = win_terms.reshape(n_blocks, 4, block_len, win_terms.shape[2], win_terms.shape[3])
    folded = jnp.zeros((n_blocks + 3,) + pieces.shape[2:], jnp.float32)
    for offset in range(4):
        folded = folded + jnp.pad(pieces[:, offset], ((offset, 3 - offset), (0, 0), (0, 0), (0, 0)))
    return (mixed_out, grad_query, folded)


def pick_rows(wanted, table_piece):
    inside = (wanted >= 0) & (wanted < table_piece.shape[0])
    picked = jnp.take(table_piece, jnp.clip(wanted, 0, table_piece.shape[0] - 1), axis=0)
    return jnp.where(inside[:, None], picked, jnp.zeros_like(picked))


def shards(
    frame_in,
    token_ids,
    durations,
    valid_len,
    t_bin,
    token_table,
    enc_weight,
    mod_table,
    w_query,
    w_key,
    w_value,
    attn_grad,
):
    frames = frame_in[0]
    n_frames = frames.shape[0]
    seq_count = lax.axis_size("seq")
    seq_index = lax.axis_index("seq")
    dp_count = lax.axis_size("dp")
    frames_total = n_frames * seq_count
    valid_end = valid_len[0]
    wanted = token_ids[0, 0]
    token_emb = pick_rows(wanted, lax.all_gather(token_table, "seq", axis=0, tiled=True))
    token_ends = jnp.cumsum(durations[0, 0])
    local_pos = jnp.arange(n_frames, dtype=jnp.int32)
    owner_tok = jnp.sum((token_ends[None, :] <= local_pos[:, None]).astype(jnp.int32), axis=1)
    frame_emb = jnp.take(token_emb, owner_tok, axis=0)
    hidden_in = frames.astype(jnp.float32) + jnp.dot(
        frame_emb, enc_weight, preferred_element_type=jnp.float32
    )
    root_ms = jnp.sqrt(jnp.mean(hidden_in * hidden_in, axis=1, keepdims=True) + 1e-06)
    normed = hidden_in / root_ms
    modulation = lax.dynamic_index_in_dim(mod_table, t_bin[0], 0, keepdims=False)
    gain_part = 1.0 + modulation[:D]
    shift_part = modulation[D:]
    modulated = (normed * gain_part + shift_part).astype(jnp.bfloat16)
    shard_cat = jnp.concatenate([w_query, w_key, w_value], axis=1)
    weights_all = lax.all_gather(shard_cat, "seq", axis=0, tiled=True)
    projected = jnp.dot(modulated, weights_all, preferred_element_type=jnp.float32).astype(
        jnp.bfloat16
    )
    queries = projected[:, :QW]
    keys_values = projected[:, QW:]
    padded = extended_2(keys_values, (("seq", 0),), 2 * BLK)
    extended = padded[: n_frames + 3 * BLK]
    n_blocks = n_frames // BLK
    ext_blocks = extended.reshape(n_blocks + 3, BLK, 2, HEADS, HD)
    global_pos = seq_index * n_frames + local_pos
    query_pos = global_pos.reshape(n_blocks, BLK)
    key_pos = (
        seq_index * n_frames
        + (jnp.arange(n_blocks, dtype=jnp.int32)[:, None] - 2) * BLK
        + jnp.arange(4 * BLK, dtype=jnp.int32)[None, :]
    )
    live_rows = global_pos < valid_end
    grad_live = jnp.where(live_rows[:, None], attn_grad[0], jnp.zeros_like(attn_grad[0]))
    attn_blocks, query_grad, ext_grad = attend_window(
        queries.reshape(n_blocks, BLK, HEADS, HD),
        ext_blocks[:, :, 0],
        ext_blocks[:, :, 1],
        grad_live.reshape(n_blocks, BLK, HEADS, HD),
        query_pos,
        key_pos,
        valid_end,
        frames_total,
    )
    ext_rows = ext_grad.reshape(n_frames + 3 * BLK, 2 * QW)
    from_next = shifted(ext_rows[: 2 * BLK], "seq", -1)
    from_prev = shifted(ext_rows[n_frames + 2 * BLK :], "seq", 1)
    own_rows = ext_rows[2 * BLK : 2 * BLK + n_frames]
    own_rows = (
        own_rows
        + jnp.pad(from_next, ((n_frames - 2 * BLK, 0), (0, 0)))
        + jnp.pad(from_prev, ((0, n_frames - BLK), (0, 0)))
    )
    grad_cat = jnp.concatenate(
        [query_grad.reshape(n_frames, QW), own_rows.astype(jnp.bfloat16)], axis=1
    )
    grad_scale = 1.0 / math.sqrt(dp_count * frames_total)
    per_seq = lax.psum_scatter(
        (
            lax.dot_general(
                modulated, grad_cat, (((0,), (0,)), ((), ())), preferred_element_type=jnp.float32
            )
            * grad_scale
        ).astype(jnp.bfloat16),
        "seq",
        scatter_dimension=0,
        tiled=True,
    ).astype(jnp.float32)
    weight_grad = lax.psum(per_seq, "dp")
    hidden_grad = lax.dot_general(
        grad_cat, weights_all, (((1,), (1,)), ((), ())), preferred_element_type=jnp.float32
    )
    scaled_grad = hidden_grad * gain_part
    frame_grad = (
        scaled_grad - normed * jnp.mean(scaled_grad * normed, axis=1, keepdims=True)
    ) / root_ms
    return (
        attn_blocks.reshape(n_frames, QW)[None],
        frame_grad.astype(jnp.bfloat16)[None],
        weight_grad[:, :QW],
        weight_grad[:, QW : 2 * QW],
        weight_grad[:, 2 * QW :],
    )


def solution(mesh):
    placed = (
        P("dp", "seq", None),
        P("dp", "seq", None),
        P("dp", "seq", None),
        P("dp"),
        P("dp"),
        P("seq", None),
        P(),
        P(),
        P("seq", None),
        P("seq", None),
        P("seq", None),
        P("dp", "seq", None),
    )
    return jax.shard_map(
        shards,
        mesh=mesh,
        in_specs=placed,
        out_specs=(
            P("dp", "seq", None),
            P("dp", "seq", None),
            P("seq", None),
            P("seq", None),
            P("seq", None),
        ),
        check_vma=False,
    )
```

profile of v0, /device:TPU:25, one launch (start us, length us, event | category | flops | bytes accessed | tf_op | source)
XLA Modules:
  0.0 553.6 jit_solution(4595249403937196069)
XLA Ops:
  7.2 0.7 all-gather.3.cloned.1.call-update
  8.0 1.4 pad_maximum_fusion.8
  10.8 0.8 copy.50
  11.6 0.1 reduce
  11.8 1.9 squeeze.30
  13.7 0.7 fusion.38
  14.5 0.9 dynamic-slice_add_fusion
  15.3 0.7 compare_and_fusion
  16.0 0.7 and_bitcast_fusion
  16.7 81.7 %all-gather.3.cloned.1.call-done = bf16[3328,512]{1,0:T(8,128)(2,1)} async-done(((bf16[104,512]{1,0:T(8,128)(2,1)}), bf16[3328,512]{1,0:T(8,128)(2,1)}) %all-gather.3.cloned.1.call-update) | async-done | bytes 3407888 | tf_op jit(solution)/shard_map/all_gather | solution.py:116
  98.5 3.1 gather_fusion
  101.7 0.9 gather_fusion.1
  102.6 0.5 multiply_reduce_fusion.2
  103.1 81.1 %all-gather.5.cloned.1.call-done = bf16[1024,1536]{1,0:T(8,128)(2,1)} async-done(((bf16[32,1536]{1,0:T(8,128)(2,1)}), bf16[1024,1536]{1,0:T(8,128)(2,1)}) %all-gather.5.cloned.1.call-update) | async-done | bytes 3145744 | tf_op jit(solution)/shard_map/all_gather | solution.py:131
  184.2 2.6 convolution_convert_fusion
  186.8 2.8 collective-permute-start
  189.7 1.5 collective-permute-start.1
  191.3 0.9 reshape.221
  192.3 3.8 collective-permute-done.1
  196.1 0.7 reshape.220
  196.9 1.5 fusion.53
  198.3 1.3 copy.72
  199.6 2.1 copy.74
  201.7 1.0 copy.73
  202.7 1.0 copy.71
  203.6 1.0 copy.70
  204.6 0.3 copy.69
  204.9 1.0 copy.68
  205.9 0.3 copy.75
  206.2 3.3 fusion.56
  209.5 2.1 convolution_bitcast_fusion
  211.6 2.0 fusion.24
  213.6 10.4 %convolution_bitcast_fusion.1 = f32[3,192,8,64]{1,3,2,0:T(8,128)} fusion(f32[3,8,48,192]{3,2,1,0:T(8,128)} %fusion.24, bf16[3,48,8,64]{3,2,1,0:T(8,128)(2,1)} %reshape.221, f32[3,8,48,192]{3,2,1,0:T(8,128)} %get-tuple-element.29, f32[3,8,48]{2,1,0:T(8,128)S(1)} %get-tuple-element.28), kind=kOutput, calls=%fused_computation.10 | convolution fusion | flops 29861184 | bytes 3101184 | tf_op jit(solution)/shard_map/bhqk,bqhd->bkhd/dot_general | solution.py:74
  224.0 3.5 pad_maximum_fusion
  227.5 5.9 %copy.64 = f32[3,192,16,64]{3,2,1,0:T(8,128)} copy(f32[3,192,16,64]{1,3,2,0:T(8,128)} %pad_maximum_fusion) | data formatting | bytes 4718592 | tf_op jit(solution)/shard_map/concatenate | solution.py:80
  233.4 2.7 slice_bitcast_fusion.3
  236.1 0.3 pad_add_fusion
  236.5 0.7 copy-done.1
  237.1 0.4 copy-done.3
  237.6 1.4 copy-done.5
  239.0 1.0 slice.179
  240.0 2.2 slice.152
  242.1 1.4 collective-permute-start.2
  243.6 0.2 copy-done.4
  243.8 0.8 pad_add_fusion.1
  244.6 1.8 slice.154
  246.4 4.5 collective-permute-start.3
  250.9 10.3 %fusion.11 = bf16[3,48,8,64]{3,1,2,0:T(8,128)(2,1)S(1)} fusion(f32[3,8,48,192]{3,2,1,0:T(8,128)} %fusion.24, bf16[3,48,8,64]{1,3,2,0:T(8,128)(2,1)} %bitcast.85, bf16[3,48,8,64]{1,3,2,0:T(8,128)(2,1)} %bitcast.80, bf16[3,48,8,64]{1,3,2,0:T(8,128)(2,1)} %bitcast.83, bf16[3,48,8,64]{1,3,2,0:T(8,128)(2,1)} %bitcast.79, ...), kind=kOutput, calls=%fused_computation.28 | convolution fusion | flops 32294208 | bytes 2511360 | tf_op jit(solution)/shard_map/bhqk,bkhd->bqhd/dot_general | solution.py:71
  261.2 0.2 reshape.222
  261.5 0.3 slice.150
  261.9 1.2 add_convert_fusion
  263.0 0.7 copy-done.23
  263.8 2.7 multiply_convert_fusion
  266.6 0.9 copy-done.11
  267.5 0.1 copy-done.13
  267.6 0.1 copy-done.15
  267.7 0.1 copy-done.17
  267.9 2.2 fusion.10
  270.1 0.9 broadcast_in_dim_reshape.4
  271.0 3.3 multiply_reduce_fusion.1
  274.3 0.9 fusion.21
  275.2 218.2 %reduce-scatter.2.cloned.1.call-done = bf16[32,1536]{1,0:T(8,128)(2,1)} async-done(((bf16[1024,1536]{1,0:T(8,128)(2,1)}), bf16[32,1536]{1,0:T(8,128)(2,1)}) %reduce-scatter.2.cloned.1.call-update) | async-done | bytes 98320 | tf_op jit(solution)/shard_map/reduce_scatter | solution.py:173
  493.4 53.0 %all-reduce.7 = f32[32,1536]{1,0:T(8,128)S(1)} all-reduce(bf16[32,1536]{1,0:T(8,128)(2,1)} %reduce-scatter.2.cloned.1.call-done), channel_id=1, replica_groups=mesh['dp'=16,'seq'=32] {'dp'}, use_global_device_ids=true, to_apply=%region_8.9 | all-reduce | flops 49152 | bytes 294912 | tf_op jit(solution)/shard_map/psum | solution.py:184
  546.4 0.7 fusion.55
  (90 shorter events, 1.1 us)
Async XLA Ops:
  7.2 95.4 %copy-start = (bf16[512,1024]{1,0:T(8,128)(2,1)S(1)}, bf16[512,1024]{1,0:T(8,128)(2,1)}, u32[]{:S(2)}) copy-start(bf16[512,1024]{1,0:T(8,128)(2,1)} %param.18) | copy-start | bytes 3145732
  7.2 91.3 %all-gather.3.cloned.1.call-start = ((), (), s32[]{:S(2)}) async-start(), calls=%async_computation.1 | async-start | bytes 3514368 | tf_op jit(solution)/shard_map/all_gather | solution.py:116
  7.9 176.3 %all-gather.5.cloned.1.call-start = ((), (), s32[]{:S(2)}) async-start(), calls=%async_computation.2 | async-start | bytes 3244032 | tf_op jit(solution)/shard_map/all_gather | solution.py:131
  9.4 484.0 %reduce-scatter.2.cloned.1.call-start = ((), (), s32[]{:S(2)}) async-start(), calls=%async_computation.3 | async-start | bytes 3244032 | tf_op jit(solution)/shard_map/reduce_scatter | solution.py:173
  11.7 90.8 %copy-start.22 = (bf16[1,144,1024]{2,1,0:T(8,128)(2,1)S(1)}, bf16[1,144,1024]{2,1,0:T(8,128)(2,1)}, u32[]{:S(2)}) copy-start(bf16[1,144,1024]{2,1,0:T(8,128)(2,1)} %param.12) | copy-start | bytes 884740
  15.3 168.9 %copy-start.24 = (f32[1,1024]{1,0:T(1,128)}, f32[1,1024]{1,0:T(1,128)S(1)}, u32[]{:S(2)}) copy-start(f32[1,1024]{1,0:T(1,128)S(1)} %get-tuple-element.17) | copy-start | bytes 12292
  15.3 168.9 %copy-start.27 = (f32[1,1024]{1,0:T(1,128)}, f32[1,1024]{1,0:T(1,128)S(1)}, u32[]{:S(2)}) copy-start(f32[1,1024]{1,0:T(1,128)S(1)} %get-tuple-element.18) | copy-start | bytes 12292
  103.1 83.7 %copy-start.6 = (f32[144,1024]{1,0:T(8,128)}, f32[144,1024]{1,0:T(8,128)S(1)}, u32[]{:S(2)}) copy-start(f32[144,1024]{1,0:T(8,128)S(1)} %get-tuple-element.27) | copy-start | bytes 1769476
  103.1 81.1 %copy-start.29 = (f32[144]{0:T(256)}, f32[144]{0:T(256)S(1)}, u32[]{:S(2)}) copy-start(f32[144]{0:T(256)S(1)} %add_sqrt_fusion) | copy-start | bytes 1732
  186.8 5.4 collective-permute-start
  189.7 6.4 %collective-permute-start.1 = (bf16[96,1024]{1,0:T(8,128)(2,1)S(1)}, bf16[96,1024]{1,0:T(8,128)(2,1)S(1)}, u32[]{:S(2)}, u32[]{:S(2)}) collective-permute-start(bf16[96,1024]{1,0:T(8,128)(2,1)S(1)} %get-tuple-element.20), channel_id=1, source_target_pairs={{1,0},{2,1},{3,2},{4,3},{5,4},{6,5},{7,6},{8,7},{9,8},{10,9},{11,1... | collective-permute-start | bytes 589832 | tf_op jit(solution)/shard_map/ppermute | solution.py:24
  198.3 3.3 copy-start.9
  198.3 4.3 copy-start.8
  199.6 6.6 %copy-start.18 = (bf16[3,48,1,8,64]{1,4,3,0,2:T(8,128)(2,1)}, bf16[3,48,1,8,64]{1,4,3,0,2:T(8,128)(2,1)S(1)}, u32[]{:S(2)}) copy-start(bf16[3,48,1,8,64]{1,4,3,0,2:T(8,128)(2,1)S(1)} %copy.72) | copy-start | bytes 442372
  204.6 1.6 copy-start.19
  204.9 6.7 %copy-start.14 = (bf16[3,48,1,8,64]{1,4,3,0,2:T(8,128)(2,1)}, bf16[3,48,1,8,64]{1,4,3,0,2:T(8,128)(2,1)S(1)}, u32[]{:S(2)}) copy-start(bf16[3,48,1,8,64]{1,4,3,0,2:T(8,128)(2,1)S(1)} %copy.69) | copy-start | bytes 442372
  206.2 3.3 copy-start.20
  209.5 4.1 copy-start.32
  209.5 2.1 copy-start.10
  209.5 2.1 copy-start.12
  209.5 2.1 copy-start.16
  209.5 2.1 copy-start.21
  236.1 1.0 copy-start.1
  236.1 1.4 copy-start.3
  237.6 1.4 copy-start.5
  242.1 1.4 copy-start.2
  242.1 1.6 copy-start.4
  242.1 19.7 %collective-permute-start.2 = (f32[96,1024]{1,0:T(8,128)}, f32[96,1024]{1,0:T(8,128)}, u32[]{:S(2)}, u32[]{:S(2)}) collective-permute-start(f32[96,1024]{1,0:T(8,128)} %slice.152), channel_id=1, source_target_pairs={{1,0},{2,1},{3,2},{4,3},{5,4},{6,5},{7,6},{8,7},{9,8},{10,9},{11,1... | collective-permute-start | bytes 1179656 | tf_op jit(solution)/shard_map/ppermute | solution.py:34
  243.8 7.1 %copy-start.33 = (f32[3,8,48]{2,1,0:T(8,128)S(1)}, f32[3,8,48]{2,1,0:T(8,128)}, u32[]{:S(2)}) copy-start(f32[3,8,48]{2,1,0:T(8,128)} %copy-done.32) | copy-start | bytes 13828
  246.4 15.5 %collective-permute-start.3 = (f32[48,1024]{1,0:T(8,128)}, f32[48,1024]{1,0:T(8,128)}, u32[]{:S(2)}, u32[]{:S(2)}) collective-permute-start(f32[48,1024]{1,0:T(8,128)} %slice.154), channel_id=1, source_target_pairs={{0,1},{1,2},{2,3},{3,4},{4,5},{5,6},{6,7},{7,8},{8,9},{9,10},{10,1... | collective-permute-start | bytes 589832 | tf_op jit(solution)/shard_map/ppermute | solution.py:34
  250.9 10.6 %slice-start = ((f32[6,48,16,64]{3,2,1,0:T(8,128)}), f32[3,48,16,64]{3,2,1,0:T(8,128)S(1)}, s32[]{:S(2)}) async-start(f32[6,48,16,64]{3,2,1,0:T(8,128)} %copy-done.5), calls=%async_computation.4 | async-start | bytes 2359296 | tf_op jit(solution)/shard_map/slice | solution.py:163
  261.4 2.3 copy-start.7
  261.8 1.9 copy-start.25
  261.8 1.9 copy-start.28
  261.8 1.9 copy-start.30
  263.0 0.7 copy-start.23
  266.5 1.0 copy-start.11
  266.5 1.1 copy-start.13
  266.5 1.2 copy-start.15
  266.5 1.3 copy-start.17
  266.5 1.3 copy-start.34
  267.9 3.2 copy-start.26
  267.9 3.2 copy-start.31
Sparse Core Ops, SparseCore 0:
  11.2 87.2 all-gather.2
  102.2 81.9 all-gather.4
  266.7 226.6 reduce-scatter.1
where the time goes:
time: 555 us; the launch traced here: 554 us
  waiting for transfers between devices  386 us (70%)
  blocking collectives  53 us (10%)
  matrix products  39.3 us (7%)
  local copies, waits for them, and re-layouts  38.3 us (7%)
  between operations  15.5 us (3%)
  other arithmetic  11.6 us (2%)
  starting transfers between devices  10.3 us (2%)
    reduce_scatter x1, waiting for transfers between devices, shards(): lax.psum_scatter((lax.dot_general(modulated, grad_cat, (((0,), (0,)), (()...  218 us
    all_gather x1, waiting for transfers between devices, shards(): lax.all_gather(token_table, 'seq', axis=0, tiled=True)  81.7 us
    all_gather x1, waiting for transfers between devices, shards(): weights_all = lax.all_gather(shard_cat, 'seq', axis=0, tiled=True)  81.1 us
    psum x1, blocking collectives, shards(): weight_grad = lax.psum(per_seq, 'dp')  53 us
    unnamed x78, local copies, waits for them, and re-layouts  12.7 us
  transfers between devices with their start and end apart: 7, of which 4 were waited for; matrix products, arithmetic and copies ran while one was open for 6% of the time, Pallas kernels for 0%

commit v1 on v0

--- a/solution.py
+++ b/solution.py
@@ -181,7 +181,7 @@
         scatter_dimension=0,
         tiled=True,
     ).astype(jnp.float32)
-    weight_grad = lax.psum(per_seq, "dp")
+    weight_grad = jnp.sum(lax.all_gather(per_seq, "dp"), axis=0)
     hidden_grad = lax.dot_general(
         grad_cat, weights_all, (((1,), (1,)), ((), ())), preferred_element_type=jnp.float32
     )

time: 555 us -> 554 us (level)
  the two profiles are of different devices: /device:TPU:25 before, /device:TPU:1 now
where the time goes in v1:
time: 554 us; the launch traced here: 553 us
  waiting for transfers between devices  435 us (79%)
  matrix products  39.3 us (7%)
  local copies, waits for them, and re-layouts  37.1 us (7%)
  between operations  15.6 us (3%)
  other arithmetic  15.2 us (3%)
  starting transfers between devices  10.4 us (2%)
    reduce_scatter x1, waiting for transfers between devices, shards(): lax.psum_scatter((lax.dot_general(modulated, grad_cat, (((0,), (0,)), (()...  227 us
    all_gather x1, waiting for transfers between devices, shards(): lax.all_gather(token_table, 'seq', axis=0, tiled=True)  82.8 us
    all_gather x1, waiting for transfers between devices, shards(): weights_all = lax.all_gather(shard_cat, 'seq', axis=0, tiled=True)  81.1 us
    all_gather x1, waiting for transfers between devices, shards(): weight_grad = jnp.sum(lax.all_gather(per_seq, 'dp'), axis=0)  39.9 us
    unnamed x78, local copies, waits for them, and re-layouts  11.4 us
  transfers between devices with their start and end apart: 8, of which 5 were waited for; matrix products, arithmetic and copies ran while one was open for 6% of the time, Pallas kernels for 0%

profile of v1, /device:TPU:1, one launch (start us, length us, event | category | flops | bytes accessed | tf_op | source)
XLA Modules:
  0.0 552.9 jit_solution(12460795125888865189)
XLA Ops:
  7.2 0.7 all-gather.5.cloned.1.call-update
  8.0 1.4 pad_maximum_fusion.8
  10.8 0.8 copy.50
  11.5 0.1 reduce-window.8
  11.6 0.1 reduce
  11.8 1.9 squeeze.30
  13.7 0.7 fusion.38
  14.3 0.1 convert_reduce_fusion
  14.4 0.9 dynamic-slice_add_fusion
  15.3 0.7 compare_and_fusion
  16.0 0.7 and_bitcast_fusion
  16.7 82.8 %all-gather.5.cloned.1.call-done = bf16[3328,512]{1,0:T(8,128)(2,1)} async-done(((bf16[104,512]{1,0:T(8,128)(2,1)}), bf16[3328,512]{1,0:T(8,128)(2,1)}) %all-gather.5.cloned.1.call-update) | async-done | bytes 3407888 | tf_op jit(solution)/shard_map/all_gather | solution.py:116
  99.6 3.1 gather_fusion
  102.8 0.9 gather_fusion.1
  103.7 0.5 multiply_reduce_fusion.2
  104.2 81.1 %all-gather.7.cloned.1.call-done = bf16[1024,1536]{1,0:T(8,128)(2,1)} async-done(((bf16[32,1536]{1,0:T(8,128)(2,1)}), bf16[1024,1536]{1,0:T(8,128)(2,1)}) %all-gather.7.cloned.1.call-update) | async-done | bytes 3145744 | tf_op jit(solution)/shard_map/all_gather | solution.py:131
  185.3 2.6 convolution_convert_fusion
  187.9 2.8 collective-permute-start
  190.8 1.5 collective-permute-start.1
  192.4 0.9 reshape.221
  193.4 3.8 collective-permute-done.1
  197.2 0.7 reshape.220
  198.0 1.4 fusion.53
  199.4 1.3 copy.72
  200.7 2.1 copy.74
  202.8 1.0 copy.73
  203.8 1.0 copy.71
  204.7 1.0 copy.70
  205.7 0.3 copy.69
  206.0 1.0 copy.68
  207.0 0.3 copy.75
  207.3 3.3 fusion.56
  210.6 2.1 convolution_bitcast_fusion
  212.8 2.0 fusion.24
  214.7 10.5 %convolution_bitcast_fusion.1 = f32[3,192,8,64]{1,3,2,0:T(8,128)} fusion(f32[3,8,48,192]{3,2,1,0:T(8,128)} %fusion.24, bf16[3,48,8,64]{3,2,1,0:T(8,128)(2,1)} %reshape.221, f32[3,8,48,192]{3,2,1,0:T(8,128)} %get-tuple-element.29, f32[3,8,48]{2,1,0:T(8,128)S(1)} %get-tuple-element.28), kind=kOutput, calls=%fused_computation.10 | convolution fusion | flops 29861184 | bytes 3101184 | tf_op jit(solution)/shard_map/bhqk,bqhd->bkhd/dot_general | solution.py:74
  225.2 3.5 pad_maximum_fusion
  228.7 5.9 %copy.64 = f32[3,192,16,64]{3,2,1,0:T(8,128)} copy(f32[3,192,16,64]{1,3,2,0:T(8,128)} %pad_maximum_fusion) | data formatting | bytes 4718592 | tf_op jit(solution)/shard_map/concatenate | solution.py:80
  234.6 2.7 slice_bitcast_fusion.3
  237.3 0.3 pad_add_fusion
  237.6 0.7 copy-done.1
  238.3 0.5 copy-done.3
  238.8 1.4 copy-done.5
  240.2 1.0 slice.179
  241.2 2.2 slice.152
  243.3 1.4 collective-permute-start.2
  244.8 0.2 copy-done.4
  244.9 0.8 pad_add_fusion.1
  245.7 1.8 slice.154
  247.5 4.5 collective-permute-start.3
  252.0 10.3 %fusion.11 = bf16[3,48,8,64]{3,1,2,0:T(8,128)(2,1)S(1)} fusion(f32[3,8,48,192]{3,2,1,0:T(8,128)} %fusion.24, bf16[3,48,8,64]{1,3,2,0:T(8,128)(2,1)} %bitcast.87, bf16[3,48,8,64]{1,3,2,0:T(8,128)(2,1)} %bitcast.82, bf16[3,48,8,64]{1,3,2,0:T(8,128)(2,1)} %bitcast.85, bf16[3,48,8,64]{1,3,2,0:T(8,128)(2,1)} %bitcast.81, ...), kind=kOutput, calls=%fused_computation.28 | convolution fusion | flops 32294208 | bytes 2511360 | tf_op jit(solution)/shard_map/bhqk,bkhd->bqhd/dot_general | solution.py:71
  262.4 0.2 reshape.222
  262.7 0.3 slice.150
  263.1 1.2 add_convert_fusion
  264.2 0.7 copy-done.23
  265.0 2.7 multiply_convert_fusion
  267.8 226.9 %reduce-scatter.2.cloned.1.call-done = bf16[32,1536]{1,0:T(8,128)(2,1)} async-done(((bf16[1024,1536]{1,0:T(8,128)(2,1)}), bf16[32,1536]{1,0:T(8,128)(2,1)}) %reduce-scatter.2.cloned.1.call-update) | async-done | bytes 98320 | tf_op jit(solution)/shard_map/reduce_scatter | solution.py:173
  494.7 1.6 all_gather.20
  496.4 2.2 fusion.10
  498.7 0.9 broadcast_in_dim_reshape.4
  499.6 3.3 multiply_reduce_fusion.1
  502.9 0.9 fusion.21
  503.8 39.9 %all-gather.9.cloned.1.call-done = f32[512,1536]{1,0:T(8,128)} async-done(((f32[32,1536]{1,0:T(8,128)}), f32[512,1536]{1,0:T(8,128)}) %all-gather.9.cloned.1.call-update) | async-done | bytes 3145744 | tf_op jit(solution)/shard_map/all_gather | solution.py:184
  543.7 2.1 reduce_sum.62
  545.7 0.7 fusion.55
  (94 shorter events, 0.9 us)
Async XLA Ops:
  7.2 96.5 %copy-start = (bf16[512,1024]{1,0:T(8,128)(2,1)S(1)}, bf16[512,1024]{1,0:T(8,128)(2,1)}, u32[]{:S(2)}) copy-start(bf16[512,1024]{1,0:T(8,128)(2,1)} %param.18) | copy-start | bytes 3145732
  7.2 92.4 %all-gather.5.cloned.1.call-start = ((), (), s32[]{:S(2)}) async-start(), calls=%async_computation.1 | async-start | bytes 3514368 | tf_op jit(solution)/shard_map/all_gather | solution.py:116
  7.9 177.4 %all-gather.7.cloned.1.call-start = ((), (), s32[]{:S(2)}) async-start(), calls=%async_computation.2 | async-start | bytes 3244032 | tf_op jit(solution)/shard_map/all_gather | solution.py:131
  9.4 485.3 %reduce-scatter.2.cloned.1.call-start = ((), (), s32[]{:S(2)}) async-start(), calls=%async_computation.3 | async-start | bytes 3244032 | tf_op jit(solution)/shard_map/reduce_scatter | solution.py:173
  11.7 91.9 %copy-start.22 = (bf16[1,144,1024]{2,1,0:T(8,128)(2,1)S(1)}, bf16[1,144,1024]{2,1,0:T(8,128)(2,1)}, u32[]{:S(2)}) copy-start(bf16[1,144,1024]{2,1,0:T(8,128)(2,1)} %param.12) | copy-start | bytes 884740
  15.3 170.0 %copy-start.24 = (f32[1,1024]{1,0:T(1,128)}, f32[1,1024]{1,0:T(1,128)S(1)}, u32[]{:S(2)}) copy-start(f32[1,1024]{1,0:T(1,128)S(1)} %get-tuple-element.17) | copy-start | bytes 12292
  15.3 170.0 %copy-start.27 = (f32[1,1024]{1,0:T(1,128)}, f32[1,1024]{1,0:T(1,128)S(1)}, u32[]{:S(2)}) copy-start(f32[1,1024]{1,0:T(1,128)S(1)} %get-tuple-element.18) | copy-start | bytes 12292
  104.2 83.7 %copy-start.6 = (f32[144,1024]{1,0:T(8,128)}, f32[144,1024]{1,0:T(8,128)S(1)}, u32[]{:S(2)}) copy-start(f32[144,1024]{1,0:T(8,128)S(1)} %get-tuple-element.27) | copy-start | bytes 1769476
  104.2 81.1 %copy-start.29 = (f32[144]{0:T(256)}, f32[144]{0:T(256)S(1)}, u32[]{:S(2)}) copy-start(f32[144]{0:T(256)S(1)} %add_sqrt_fusion) | copy-start | bytes 1732
  187.9 5.4 collective-permute-start
  190.8 6.4 %collective-permute-start.1 = (bf16[96,1024]{1,0:T(8,128)(2,1)S(1)}, bf16[96,1024]{1,0:T(8,128)(2,1)S(1)}, u32[]{:S(2)}, u32[]{:S(2)}) collective-permute-start(bf16[96,1024]{1,0:T(8,128)(2,1)S(1)} %get-tuple-element.20), channel_id=1, source_target_pairs={{1,0},{2,1},{3,2},{4,3},{5,4},{6,5},{7,6},{8,7},{9,8},{10,9},{11,1... | collective-permute-start | bytes 589832 | tf_op jit(solution)/shard_map/ppermute | solution.py:24
  199.4 3.4 copy-start.9
  199.4 4.4 copy-start.8
  200.7 6.6 %copy-start.18 = (bf16[3,48,1,8,64]{1,4,3,0,2:T(8,128)(2,1)}, bf16[3,48,1,8,64]{1,4,3,0,2:T(8,128)(2,1)S(1)}, u32[]{:S(2)}) copy-start(bf16[3,48,1,8,64]{1,4,3,0,2:T(8,128)(2,1)S(1)} %copy.72) | copy-start | bytes 442372
  205.7 1.6 copy-start.19
  206.0 6.7 %copy-start.14 = (bf16[3,48,1,8,64]{1,4,3,0,2:T(8,128)(2,1)}, bf16[3,48,1,8,64]{1,4,3,0,2:T(8,128)(2,1)S(1)}, u32[]{:S(2)}) copy-start(bf16[3,48,1,8,64]{1,4,3,0,2:T(8,128)(2,1)S(1)} %copy.69) | copy-start | bytes 442372
  207.3 3.3 copy-start.20
  210.6 4.1 copy-start.32
  210.6 2.1 copy-start.10
  210.6 2.1 copy-start.12
  210.6 2.1 copy-start.16
  210.6 2.1 copy-start.21
  237.3 1.0 copy-start.1
  237.3 1.4 copy-start.3
  238.8 1.4 copy-start.5
  243.3 1.4 copy-start.2
  243.3 1.6 copy-start.4
  243.3 19.7 %collective-permute-start.2 = (f32[96,1024]{1,0:T(8,128)}, f32[96,1024]{1,0:T(8,128)}, u32[]{:S(2)}, u32[]{:S(2)}) collective-permute-start(f32[96,1024]{1,0:T(8,128)} %slice.152), channel_id=1, source_target_pairs={{1,0},{2,1},{3,2},{4,3},{5,4},{6,5},{7,6},{8,7},{9,8},{10,9},{11,1... | collective-permute-start | bytes 1179656 | tf_op jit(solution)/shard_map/ppermute | solution.py:34
  244.9 7.1 %copy-start.33 = (f32[3,8,48]{2,1,0:T(8,128)S(1)}, f32[3,8,48]{2,1,0:T(8,128)}, u32[]{:S(2)}) copy-start(f32[3,8,48]{2,1,0:T(8,128)} %copy-done.32) | copy-start | bytes 13828
  247.5 15.5 %collective-permute-start.3 = (f32[48,1024]{1,0:T(8,128)}, f32[48,1024]{1,0:T(8,128)}, u32[]{:S(2)}, u32[]{:S(2)}) collective-permute-start(f32[48,1024]{1,0:T(8,128)} %slice.154), channel_id=1, source_target_pairs={{0,1},{1,2},{2,3},{3,4},{4,5},{5,6},{6,7},{7,8},{8,9},{9,10},{10,1... | collective-permute-start | bytes 589832 | tf_op jit(solution)/shard_map/ppermute | solution.py:34
  252.0 10.6 %slice-start = ((f32[6,48,16,64]{3,2,1,0:T(8,128)}), f32[3,48,16,64]{3,2,1,0:T(8,128)S(1)}, s32[]{:S(2)}) async-start(f32[6,48,16,64]{3,2,1,0:T(8,128)} %copy-done.5), calls=%async_computation.5 | async-start | bytes 2359296 | tf_op jit(solution)/shard_map/slice | solution.py:163
  262.7 2.3 copy-start.7
  263.0 1.9 copy-start.25
  263.0 1.9 copy-start.28
  263.0 1.9 copy-start.30
  264.2 0.7 copy-start.23
  267.7 228.6 %copy-start.11 = (bf16[3,48,1,8,64]{1,4,3,0,2:T(8,128)(2,1)S(1)}, bf16[3,48,1,8,64]{1,4,3,0,2:T(8,128)(2,1)}, u32[]{:S(2)}) copy-start(bf16[3,48,1,8,64]{1,4,3,0,2:T(8,128)(2,1)} %copy.71) | copy-start | bytes 442372
  267.7 228.7 %copy-start.13 = (bf16[3,48,1,8,64]{1,4,3,0,2:T(8,128)(2,1)S(1)}, bf16[3,48,1,8,64]{1,4,3,0,2:T(8,128)(2,1)}, u32[]{:S(2)}) copy-start(bf16[3,48,1,8,64]{1,4,3,0,2:T(8,128)(2,1)} %copy.70) | copy-start | bytes 442372
  267.7 228.7 %copy-start.15 = (bf16[3,48,1,8,64]{1,4,3,0,2:T(8,128)(2,1)S(1)}, bf16[3,48,1,8,64]{1,4,3,0,2:T(8,128)(2,1)}, u32[]{:S(2)}) copy-start(bf16[3,48,1,8,64]{1,4,3,0,2:T(8,128)(2,1)} %copy-done.14) | copy-start | bytes 442372
  267.7 228.7 %copy-start.17 = (bf16[3,48,1,8,64]{1,4,3,0,2:T(8,128)(2,1)S(1)}, bf16[3,48,1,8,64]{1,4,3,0,2:T(8,128)(2,1)}, u32[]{:S(2)}) copy-start(bf16[3,48,1,8,64]{1,4,3,0,2:T(8,128)(2,1)} %copy.68) | copy-start | bytes 442372
  267.7 228.7 %copy-start.34 = (f32[3,8,48]{2,1,0:T(8,128)S(1)}, f32[3,8,48]{2,1,0:T(8,128)}, u32[]{:S(2)}) copy-start(f32[3,8,48]{2,1,0:T(8,128)} %copy-done.32) | copy-start | bytes 13828
  267.8 275.9 %all-gather.9.cloned.1.call-start = ((), (), s32[]{:S(2)}) async-start(), calls=%async_computation.4 | async-start | bytes 3342336 | tf_op jit(solution)/shard_map/all_gather | solution.py:184
  496.4 3.2 copy-start.26
  496.4 3.2 copy-start.31
Sparse Core Ops, SparseCore 0:
  11.2 88.3 all-gather.4
  103.3 81.9 all-gather.6
  267.9 226.8 reduce-scatter.1
  496.9 46.6 all-gather.8
